TPU v7x, 32 devices: a whole 2x2x4 slice. The times are simulated.
32 devices in a mesh: dp: 8 (over z, core), ctx: 4 (over y, x).
Axes of the slice: x: 2, y: 2, z: 4, core: 2. Of those that a mesh axis runs over, the one named last changes fastest.
Arguments:
- queries: bfloat16 [8, 1536, 1024], P('dp', 'ctx'), may hold values from -32 to 32
- keys: bfloat16 [8, 1536, 1024], P('dp', 'ctx'), may hold values from -32 to 32
- values: bfloat16 [8, 1536, 1024], P('dp', 'ctx'), may hold values from -6 to 6
- out_weight: bfloat16 [2048, 1024], replicated, may hold values from -0.1875 to 0.1875
- out_cot: bfloat16 [8, 1536, 2048], P('dp', 'ctx'), may hold values from -6 to 6
- block_list: int32 [12, 8], replicated, may hold values from 0 to 11, as said below
Outputs:
- attended: bfloat16 [8, 1536, 2048], P('dp', 'ctx')
- query_gradient: bfloat16 [8, 1536, 1024], P('dp', 'ctx')
- key_grad: bfloat16 [8, 1536, 1024], P('dp', 'ctx')
- value_grad: bfloat16 [8, 1536, 1024], P('dp', 'ctx')
- weight_grad: float32 [2048, 1024], P(('dp', 'ctx'))
Inputs may be any that keep to these rules, and one draw needn't show every extreme that they name: `block_list`: row i names 8 different blocks: i - 1, i and i + 1 modulo 12, then the 2 global blocks (the same in every row) where they are not among those three, then other blocks at random.
All inputs are finite; a program needn't handle non-finite values.
Results may differ from a plain program's by a relative error of at most 0.015.
Values may be sent and summed in bfloat16 or wider, within the bound.
A program may use at most 128 MiB of HBM per device.

v0:
```python
import math

import jax
import jax.numpy as jnp
from jax import lax
from jax.sharding import PartitionSpec as P

HEADS = 8
HEAD_SIZE = 128
BLOCK_TOKENS = 128
CHOSEN_BLOCKS = 8


def block_rows(source_table, picked):
    gathered = source_table[picked.reshape(-1)]
    return gathered.reshape(
        (picked.shape[0], CHOSEN_BLOCKS * BLOCK_TOKENS) + source_table.shape[2:]
    )


def shards(queries, keys, values, out_weight, out_cot, block_list):
    tokens = queries.shape[1]
    head_cols = queries.shape[2]
    n_ctx = lax.axis_size("ctx")
    n_dp = lax.axis_size("dp")
    local_heads = HEADS // n_ctx
    inverse_root_scale = 1.0 / math.sqrt(HEAD_SIZE)

    def by_head(matrix):
        return matrix[0].reshape(tokens, HEADS, HEAD_SIZE)

    query_heads, key_heads, value_heads = (
        lax.all_to_all(by_head(queries), "ctx", split_axis=1, concat_axis=0, tiled=True),
        lax.all_to_all(by_head(keys), "ctx", split_axis=1, concat_axis=0, tiled=True),
        lax.all_to_all(by_head(values), "ctx", split_axis=1, concat_axis=0, tiled=True),
    )
    length = query_heads.shape[0]
    block_total = length // BLOCK_TOKENS
    group_len = math.gcd(block_total, max(1, 512 // BLOCK_TOKENS))
    step_count = block_total // group_len
    key_table = key_heads.reshape(block_total, BLOCK_TOKENS, local_heads, HEAD_SIZE)
    value_table = value_heads.reshape(block_total, BLOCK_TOKENS, local_heads, HEAD_SIZE)
    query_groups = query_heads.reshape(step_count, group_len, BLOCK_TOKENS, local_heads, HEAD_SIZE)
    pick_groups = block_list.reshape(step_count, group_len, CHOSEN_BLOCKS)

    def forward_step(inputs):
        query_part, picked = inputs
        chosen_keys = block_rows(key_table, picked)
        chosen_values = block_rows(value_table, picked)
        logit_scores = (
            jnp.einsum(
                "gqhd,gkhd->ghqk", query_part, chosen_keys, preferred_element_type=jnp.float32
            )
            * inverse_root_scale
        )
        row_max = jnp.max(logit_scores, axis=-1, keepdims=True)
        expo_rows = jnp.exp(logit_scores - row_max)
        row_sum = jnp.sum(expo_rows, axis=-1, keepdims=True)
        weight_matrix = (expo_rows / row_sum).astype(jnp.bfloat16)
        result = jnp.einsum(
            "ghqk,gkhd->gqhd", weight_matrix, chosen_values, preferred_element_type=jnp.float32
        ).astype(jnp.bfloat16)
        return (result, (row_max + jnp.log(row_sum))[..., 0])

    attn_groups, log_total = lax.map(forward_step, (query_groups, pick_groups))
    attn_heads = attn_groups.reshape(length, local_heads, HEAD_SIZE)
    attn_seq = lax.all_to_all(attn_heads, "ctx", split_axis=0, concat_axis=1, tiled=True).reshape(
        tokens, head_cols
    )
    attended = jnp.dot(attn_seq, out_weight.T, preferred_element_type=jnp.float32).astype(
        jnp.bfloat16
    )
    cot_rows = out_cot[0]
    attn_cot = jnp.dot(cot_rows, out_weight, preferred_element_type=jnp.float32).astype(
        jnp.bfloat16
    )
    cot_heads = lax.all_to_all(
        attn_cot.reshape(tokens, HEADS, HEAD_SIZE), "ctx", split_axis=1, concat_axis=0, tiled=True
    )
    weight_sum = lax.psum_scatter(
        lax.dot_general(
            cot_rows, attn_seq, (((0,), (0,)), ((), ())), preferred_element_type=jnp.float32
        ),
        ("dp", "ctx"),
        scatter_dimension=0,
        tiled=True,
    )
    weight_grad = weight_sum / n_dp
    row_dot = jnp.sum(cot_heads.astype(jnp.float32) * attn_heads.astype(jnp.float32), axis=-1)
    row_dot = row_dot.reshape(step_count, group_len, BLOCK_TOKENS, local_heads).transpose(
        0, 1, 3, 2
    )
    cot_groups = cot_heads.reshape(step_count, group_len, BLOCK_TOKENS, local_heads, HEAD_SIZE)

    def backward_step(running, inputs):
        key_acc, value_acc = running
        query_part, cot_part, total_part, dot_part, picked = inputs
        chosen_keys = block_rows(key_table, picked)
        chosen_values = block_rows(value_table, picked)
        flat_picks = picked.reshape(-1)
        logit_scores = (
            jnp.einsum(
                "gqhd,gkhd->ghqk", query_part, chosen_keys, preferred_element_type=jnp.float32
            )
            * inverse_root_scale
        )
        probs = jnp.exp(logit_scores - total_part[..., None])
        probs_narrow = probs.astype(jnp.bfloat16)
        value_grad_terms = jnp.einsum(
            "ghqk,gqhd->gkhd", probs_narrow, cot_part, preferred_element_type=jnp.float32
        )
        value_acc = value_acc.at[flat_picks].add(
            value_grad_terms.reshape(flat_picks.shape[0], BLOCK_TOKENS, local_heads, HEAD_SIZE)
        )
        cotangent_probs = jnp.einsum(
            "gqhd,gkhd->ghqk", cot_part, chosen_values, preferred_element_type=jnp.float32
        )
        score_cotangent = (probs * (cotangent_probs - dot_part[..., None])).astype(jnp.bfloat16)
        query_gradient = (
            jnp.einsum(
                "ghqk,gkhd->gqhd", score_cotangent, chosen_keys, preferred_element_type=jnp.float32
            )
            * inverse_root_scale
        ).astype(jnp.bfloat16)
        key_grad_terms = jnp.einsum(
            "ghqk,gqhd->gkhd", score_cotangent, query_part, preferred_element_type=jnp.float32
        )
        key_acc = key_acc.at[flat_picks].add(
            key_grad_terms.reshape(flat_picks.shape[0], BLOCK_TOKENS, local_heads, HEAD_SIZE)
        )
        return ((key_acc, value_acc), query_gradient)

    zero_table = jnp.zeros((block_total, BLOCK_TOKENS, local_heads, HEAD_SIZE), jnp.float32)
    sums_out, query_groups_grad = lax.scan(
        backward_step,
        (zero_table, zero_table),
        (query_groups, cot_groups, log_total, row_dot, pick_groups),
    )
    key_acc, value_acc = sums_out
    query_grad_heads = query_groups_grad.reshape(length, local_heads, HEAD_SIZE)
    key_grad_heads = (
        (key_acc * inverse_root_scale).astype(jnp.bfloat16).reshape(length, local_heads, HEAD_SIZE)
    )
    value_grad_heads = value_acc.astype(jnp.bfloat16).reshape(length, local_heads, HEAD_SIZE)
    query_back, key_back, value_back = (
        lax.all_to_all(query_grad_heads, "ctx", split_axis=0, concat_axis=1, tiled=True),
        lax.all_to_all(key_grad_heads, "ctx", split_axis=0, concat_axis=1, tiled=True),
        lax.all_to_all(value_grad_heads, "ctx", split_axis=0, concat_axis=1, tiled=True),
    )
    return (
        attended[None],
        query_back.reshape(1, tokens, head_cols),
        key_back.reshape(1, tokens, head_cols),
        value_back.reshape(1, tokens, head_cols),
        weight_grad,
    )


def solution(mesh):
    return jax.shard_map(
        shards,
        mesh=mesh,
        in_specs=(
            P("dp", "ctx", None),
            P("dp", "ctx", None),
            P("dp", "ctx", None),
            P(),
            P("dp", "ctx", None),
            P(),
        ),
        out_specs=(
            P("dp", "ctx", None),
            P("dp", "ctx", None),
            P("dp", "ctx", None),
            P("dp", "ctx", None),
            P(("dp", "ctx"), None),
        ),
        check_vma=False,
    )
```

profile of v0, /device:TPU:14, one launch (start us, length us, event | category | flops | bytes accessed | tf_op | source)
XLA Modules:
  0.0 460.8 jit_solution(4302018031664678899)
XLA Ops:
  15.0 8.2 %all-to-all-done.1 = bf16[384,8,128]{0,2,1:T(8,128)(2,1)S(1)} async-done(((bf16[384,8,128]{0,2,1:T(8,128)(2,1)}), bf16[384,8,128]{0,2,1:T(8,128)(2,1)S(1)}, u32[]{:S(2)}, u32[]{:S(2)}) %all-to-all-start.1) | async-done | bytes 786464 | tf_op jit(solution)/shard_map/all_to_all | solution.py:33
  30.6 6.5 %all-to-all-done.2 = bf16[384,8,128]{0,2,1:T(8,128)(2,1)S(1)} async-done(((bf16[384,8,128]{0,2,1:T(8,128)(2,1)}), bf16[384,8,128]{0,2,1:T(8,128)(2,1)S(1)}, u32[]{:S(2)}, u32[]{:S(2)}) %all-to-all-start.2) | async-done | bytes 786464 | tf_op jit(solution)/shard_map/all_to_all | solution.py:34
  56.9 62.3 %while.26 = (s32[]{:T(128)}, bf16[3,4,128,2,128]{4,2,1,0,3:T(8,128)(2,1)}, f32[3,4,2,128]{3,2,1,0:T(2,128)S(1)}, s32[3,4,8]{2,1,0:T(4,128)S(1)}, bf16[12,128,2,1...) while((s32[]{:T(128)}, ...), condition=%wide.region_3.4_spmd, body=%wide.region_0.3_spmd.sunk | while | flops 546439296 | bytes 35165448 | solution.py:65
  57.2 6.2 %gather_fusion.1 = bf16[32,128,2,128]{3,2,1,0:T(2,128)(2,1)} fusion(bf16[12,128,2,128]{3,2,1,0:T(2,128)(2,1)S(1)} %get-tuple-element.405, s32[1024]{0:T(1024)S(1)} %pad_clamp_fusion.4), kind=kCustom, calls=%fused_computation.clone.1 | custom fusion | bytes 4194432 | tf_op jit(solution)/shard_map/while/body/eval_jaxpr/gather | solution.py:15
  63.4 6.2 %gather_fusion = bf16[32,128,2,128]{3,2,1,0:T(2,128)(2,1)} fusion(bf16[12,128,2,128]{3,2,1,0:T(2,128)(2,1)S(1)} %get-tuple-element.407, s32[1024]{0:T(1024)S(1)} %pad_clamp_fusion.4), kind=kCustom, calls=%fused_computation.1.clone.1 | custom fusion | bytes 4194432 | tf_op jit(solution)/shard_map/while/body/eval_jaxpr/gather | solution.py:15
  77.9 6.2 %gather_fusion.1 = bf16[32,128,2,128]{3,2,1,0:T(2,128)(2,1)} fusion(bf16[12,128,2,128]{3,2,1,0:T(2,128)(2,1)S(1)} %get-tuple-element.405, s32[1024]{0:T(1024)S(1)} %pad_clamp_fusion.4), kind=kCustom, calls=%fused_computation.clone.1 | custom fusion | bytes 4194432 | tf_op jit(solution)/shard_map/while/body/eval_jaxpr/gather | solution.py:15
  84.1 6.2 %gather_fusion = bf16[32,128,2,128]{3,2,1,0:T(2,128)(2,1)} fusion(bf16[12,128,2,128]{3,2,1,0:T(2,128)(2,1)S(1)} %get-tuple-element.407, s32[1024]{0:T(1024)S(1)} %pad_clamp_fusion.4), kind=kCustom, calls=%fused_computation.1.clone.1 | custom fusion | bytes 4194432 | tf_op jit(solution)/shard_map/while/body/eval_jaxpr/gather | solution.py:15
  98.6 6.2 %gather_fusion.1 = bf16[32,128,2,128]{3,2,1,0:T(2,128)(2,1)} fusion(bf16[12,128,2,128]{3,2,1,0:T(2,128)(2,1)S(1)} %get-tuple-element.405, s32[1024]{0:T(1024)S(1)} %pad_clamp_fusion.4), kind=kCustom, calls=%fused_computation.clone.1 | custom fusion | bytes 4194432 | tf_op jit(solution)/shard_map/while/body/eval_jaxpr/gather | solution.py:15
  104.8 6.2 %gather_fusion = bf16[32,128,2,128]{3,2,1,0:T(2,128)(2,1)} fusion(bf16[12,128,2,128]{3,2,1,0:T(2,128)(2,1)S(1)} %get-tuple-element.407, s32[1024]{0:T(1024)S(1)} %pad_clamp_fusion.4), kind=kCustom, calls=%fused_computation.1.clone.1 | custom fusion | bytes 4194432 | tf_op jit(solution)/shard_map/while/body/eval_jaxpr/gather | solution.py:15
  119.2 6.7 %copy.208 = bf16[1536,2,128]{2,1,0:T(2,128)(2,1)S(1)} copy(bf16[1536,2,128]{2,0,1:T(8,128)(2,1)} %bitcast.166) | data formatting | bytes 1572864 | tf_op jit(solution)/shard_map/reshape | solution.py:66
  125.9 13.2 %all_to_all.120 = bf16[1536,2,128]{2,1,0:T(2,128)(2,1)S(1)} all-to-all(bf16[1536,2,128]{2,1,0:T(2,128)(2,1)S(1)} %copy.208), channel_id=1, replica_groups=mesh['dp'=8,'ctx'=4] {'ctx'}, dimensions={0} | all-to-all | bytes 1572864 | tf_op jit(solution)/shard_map/all_to_all | solution.py:67
  142.4 6.7 %convolution_bitcast_fusion.2 = f32[2048,1024]{0,1:T(8,128)} fusion(bf16[384,1024]{0,1:T(8,128)(2,1)} %bitcast.188, bf16[1,384,2048]{2,1,0:T(8,128)(2,1)S(1)} %copy-done), kind=kOutput, calls=%fused_computation.55 | convolution fusion | flops 1610612736 | bytes 10747904 | tf_op jit(solution)/shard_map/dot_general | solution.py:81
  149.1 9.3 %copy.242 = f32[2048,1024]{1,0:T(8,128)} copy(f32[2048,1024]{0,1:T(8,128)} %convolution_bitcast_fusion.2) | data formatting | bytes 16777216
  162.5 23.1 %all_to_all.121 = bf16[384,8,128]{2,0,1:T(8,128)(2,1)S(1)} all-to-all(bf16[384,8,128]{2,0,1:T(8,128)(2,1)S(1)} %bitcast.179), channel_id=1, replica_groups=mesh['dp'=8,'ctx'=4] {'ctx'}, dimensions={1} | all-to-all | bytes 1572864 | tf_op jit(solution)/shard_map/all_to_all | solution.py:77
  189.6 210.5 %while.27 = (s32[]{:T(128)}, f32[12,128,2,128]{3,1,2,0:T(8,128)}, f32[12,128,2,128]{3,1,2,0:T(8,128)S(1)}, bf16[3,4,128,2,128]{4,2,1,0,3:T(8,128)(2,1)}, s32[3,4...) while((s32[]{:T(128)}, f32[12,128,2,128]{3,1,2,0:T(8,128)}, ...), condition=%wide.region_8.9_spmd, body=%wide.region_5.8_spmd.sunk | while | flops 1352926336 | bytes 135571088 | solution.py:134
  195.9 6.1 %gather_fusion.2 = bf16[32,128,2,128]{3,2,1,0:T(2,128)(2,1)} fusion(bf16[12,128,2,128]{3,2,1,0:T(2,128)(2,1)S(1)} %get-tuple-element.439, s32[1024]{0:T(1024)S(1)} %pad_clamp_fusion.5), kind=kCustom, calls=%fused_computation.2.clone.1 | custom fusion | bytes 4194432 | tf_op jit(solution)/shard_map/while/body/eval_jaxpr/gather | solution.py:15
  202.0 6.2 %copy.297 = bf16[4,1024,2,128]{1,3,2,0:T(8,128)(2,1)} copy(bf16[4,1024,2,128]{3,2,1,0:T(2,128)(2,1)} %bitcast.163) | data formatting | bytes 4194304 | tf_op jit(solution)/shard_map/while/body/eval_jaxpr/reshape | solution.py:16
  226.5 6.5 %scatter_fusion.1 = f32[12,128,2,128]{3,1,2,0:T(8,128)S(1)} fusion(f32[12,128,2,128]{3,1,2,0:T(8,128)S(1)} %get-tuple-element.423, s32[32]{0:T(128)S(1)} %fusion.80, f32[32,128,2,128]{3,1,2,0:T(8,128)} %copy.301), kind=kCustom, calls=%fused_computation.5.clone.1 | custom fusion | flops 1048576 | bytes 12583040 | tf_op jit(solution)/shard_map/while/body/eval_jaxpr/scatter-add | solution.py:112
  250.0 9.8 %scatter_fusion = f32[12,128,2,128]{3,1,2,0:T(8,128)} fusion(f32[12,128,2,128]{3,1,2,0:T(8,128)} %get-tuple-element.422, s32[32]{0:T(128)S(1)} %fusion.80, f32[32,128,2,128]{3,1,2,0:T(8,128)} %copy.299), kind=kCustom, calls=%fused_computation.4.clone.1 | custom fusion | flops 1048576 | bytes 12583040 | tf_op jit(solution)/shard_map/while/body/eval_jaxpr/scatter-add | solution.py:128
  266.1 6.1 %gather_fusion.2 = bf16[32,128,2,128]{3,2,1,0:T(2,128)(2,1)} fusion(bf16[12,128,2,128]{3,2,1,0:T(2,128)(2,1)S(1)} %get-tuple-element.439, s32[1024]{0:T(1024)S(1)} %pad_clamp_fusion.5), kind=kCustom, calls=%fused_computation.2.clone.1 | custom fusion | bytes 4194432 | tf_op jit(solution)/shard_map/while/body/eval_jaxpr/gather | solution.py:15
  272.2 6.2 %copy.297 = bf16[4,1024,2,128]{1,3,2,0:T(8,128)(2,1)} copy(bf16[4,1024,2,128]{3,2,1,0:T(2,128)(2,1)} %bitcast.163) | data formatting | bytes 4194304 | tf_op jit(solution)/shard_map/while/body/eval_jaxpr/reshape | solution.py:16
  296.7 6.5 %scatter_fusion.1 = f32[12,128,2,128]{3,1,2,0:T(8,128)S(1)} fusion(f32[12,128,2,128]{3,1,2,0:T(8,128)S(1)} %get-tuple-element.423, s32[32]{0:T(128)S(1)} %fusion.80, f32[32,128,2,128]{3,1,2,0:T(8,128)} %copy.301), kind=kCustom, calls=%fused_computation.5.clone.1 | custom fusion | flops 1048576 | bytes 12583040 | tf_op jit(solution)/shard_map/while/body/eval_jaxpr/scatter-add | solution.py:112
  320.2 9.8 %scatter_fusion = f32[12,128,2,128]{3,1,2,0:T(8,128)} fusion(f32[12,128,2,128]{3,1,2,0:T(8,128)} %get-tuple-element.422, s32[32]{0:T(128)S(1)} %fusion.80, f32[32,128,2,128]{3,1,2,0:T(8,128)} %copy.299), kind=kCustom, calls=%fused_computation.4.clone.1 | custom fusion | flops 1048576 | bytes 12583040 | tf_op jit(solution)/shard_map/while/body/eval_jaxpr/scatter-add | solution.py:128
  330.2 6.1 %gather_fusion.3 = bf16[32,128,2,128]{3,2,1,0:T(2,128)(2,1)} fusion(bf16[12,128,2,128]{3,2,1,0:T(2,128)(2,1)S(1)} %get-tuple-element.442, s32[1024]{0:T(1024)S(1)} %pad_clamp_fusion.5), kind=kCustom, calls=%fused_computation.3.clone.1 | custom fusion | bytes 4194432 | tf_op jit(solution)/shard_map/while/body/eval_jaxpr/gather | solution.py:15
  336.3 6.2 %gather_fusion.2 = bf16[32,128,2,128]{3,2,1,0:T(2,128)(2,1)} fusion(bf16[12,128,2,128]{3,2,1,0:T(2,128)(2,1)S(1)} %get-tuple-element.439, s32[1024]{0:T(1024)S(1)} %pad_clamp_fusion.5), kind=kCustom, calls=%fused_computation.2.clone.1 | custom fusion | bytes 4194432 | tf_op jit(solution)/shard_map/while/body/eval_jaxpr/gather | solution.py:15
  342.5 6.2 %copy.297 = bf16[4,1024,2,128]{1,3,2,0:T(8,128)(2,1)} copy(bf16[4,1024,2,128]{3,2,1,0:T(2,128)(2,1)} %bitcast.163) | data formatting | bytes 4194304 | tf_op jit(solution)/shard_map/while/body/eval_jaxpr/reshape | solution.py:16
  366.9 6.5 %scatter_fusion.1 = f32[12,128,2,128]{3,1,2,0:T(8,128)S(1)} fusion(f32[12,128,2,128]{3,1,2,0:T(8,128)S(1)} %get-tuple-element.423, s32[32]{0:T(128)S(1)} %fusion.80, f32[32,128,2,128]{3,1,2,0:T(8,128)} %copy.301), kind=kCustom, calls=%fused_computation.5.clone.1 | custom fusion | flops 1048576 | bytes 12583040 | tf_op jit(solution)/shard_map/while/body/eval_jaxpr/scatter-add | solution.py:112
  390.3 9.6 %scatter_fusion = f32[12,128,2,128]{3,1,2,0:T(8,128)} fusion(f32[12,128,2,128]{3,1,2,0:T(8,128)} %get-tuple-element.422, s32[32]{0:T(128)S(1)} %fusion.80, f32[32,128,2,128]{3,1,2,0:T(8,128)} %copy.299), kind=kCustom, calls=%fused_computation.4.clone.1 | custom fusion | flops 1048576 | bytes 12583040 | tf_op jit(solution)/shard_map/while/body/eval_jaxpr/scatter-add | solution.py:128
  400.1 7.6 %copy.222 = bf16[1536,2,128]{2,1,0:T(2,128)(2,1)} copy(bf16[1536,2,128]{2,0,1:T(8,128)(2,1)} %bitcast.173) | data formatting | bytes 1572864 | tf_op jit(solution)/shard_map/reshape | solution.py:140
  407.7 7.0 %all-to-all-start.5 = ((bf16[1536,2,128]{2,1,0:T(2,128)(2,1)}), bf16[1536,2,128]{2,1,0:T(2,128)(2,1)}, u32[]{:S(2)}, u32[]{:S(2)}) async-start(bf16[1536,2,128]{2,1,0:T(2,128)(2,1)} %copy.222), calls=%async_computation.5 | async-start | bytes 1572864 | tf_op jit(solution)/shard_map/all_to_all | solution.py:146
  414.9 7.3 %copy.226 = bf16[1536,2,128]{2,1,0:T(2,128)(2,1)} copy(bf16[1536,2,128]{2,0,1:T(8,128)(2,1)S(1)} %bitcast.186) | data formatting | bytes 1572864 | tf_op jit(solution)/shard_map/reshape | solution.py:142
  426.5 7.3 %copy.230 = bf16[1536,2,128]{2,1,0:T(2,128)(2,1)} copy(bf16[1536,2,128]{2,0,1:T(8,128)(2,1)S(1)} %bitcast.187) | data formatting | bytes 1572864 | tf_op jit(solution)/shard_map/reshape | solution.py:144
  (178 shorter events, 214.2 us)
Async XLA Ops:
  7.2 135.2 %copy-start = (bf16[1,384,2048]{2,1,0:T(8,128)(2,1)S(1)}, bf16[1,384,2048]{2,1,0:T(8,128)(2,1)}, u32[]{:S(2)}) copy-start(bf16[1,384,2048]{2,1,0:T(8,128)(2,1)} %param.14) | copy-start | bytes 4718596
  7.2 6.6 %copy-start.10 = (bf16[1,384,1024]{2,1,0:T(8,128)(2,1)S(1)}, bf16[1,384,1024]{2,1,0:T(8,128)(2,1)}, u32[]{:S(2)}) copy-start(bf16[1,384,1024]{2,1,0:T(8,128)(2,1)} %param.11) | copy-start | bytes 2359300
  9.6 13.5 %all-to-all-start.1 = ((bf16[384,8,128]{0,2,1:T(8,128)(2,1)}), bf16[384,8,128]{0,2,1:T(8,128)(2,1)S(1)}, u32[]{:S(2)}, u32[]{:S(2)}) async-start(bf16[384,8,128]{0,2,1:T(8,128)(2,1)} %bitcast.25), calls=%async_computation.1 | async-start | bytes 1572864 | tf_op jit(solution)/shard_map/all_to_all | solution.py:33
  23.2 19.6 %copy-start.11 = (s32[12,8]{0,1:T(8,128)S(1)}, s32[12,8]{0,1:T(8,128)}, u32[]{:S(2)}) copy-start(s32[12,8]{0,1:T(8,128)} %param.15) | copy-start | bytes 1156
  23.2 13.9 %all-to-all-start.2 = ((bf16[384,8,128]{0,2,1:T(8,128)(2,1)}), bf16[384,8,128]{0,2,1:T(8,128)(2,1)S(1)}, u32[]{:S(2)}, u32[]{:S(2)}) async-start(bf16[384,8,128]{0,2,1:T(8,128)(2,1)} %bitcast.174), calls=%async_computation.2 | async-start | bytes 1572864 | tf_op jit(solution)/shard_map/all_to_all | solution.py:34
  37.1 14.5 %all-to-all-start = ((bf16[384,8,128]{0,2,1:T(8,128)(2,1)}), bf16[384,8,128]{0,2,1:T(8,128)(2,1)}, u32[]{:S(2)}, u32[]{:S(2)}) async-start(bf16[384,8,128]{0,2,1:T(8,128)(2,1)} %bitcast.172), calls=%async_computation | async-start | bytes 1572864 | tf_op jit(solution)/shard_map/all_to_all | solution.py:35
  42.7 408.9 %reduce-scatter.4.cloned.1.call-start = ((), (), s32[]{:S(2)}) async-start(), calls=%async_computation.9 | async-start | bytes 8650752
  72.0 1.6 copy-start.6
  92.7 1.6 copy-start.6
  113.4 1.6 copy-start.6
  162.3 24.2 %copy-start.8 = (bf16[3,4,128,2,128]{4,2,1,0,3:T(8,128)(2,1)S(1)}, bf16[3,4,128,2,128]{4,2,1,0,3:T(8,128)(2,1)}, u32[]{:S(2)}) copy-start(bf16[3,4,128,2,128]{4,2,1,0,3:T(8,128)(2,1)} %get-tuple-element.102) | copy-start | bytes 2359300
  208.2 2.5 copy-start.5
  208.2 2.5 copy-start.7
  210.8 1.6 copy-start.3
  212.4 1.3 copy-start.2
  278.4 2.5 copy-start.5
  278.4 2.5 copy-start.7
  280.9 1.6 copy-start.3
  282.6 1.3 copy-start.2
  348.6 2.5 copy-start.5
  348.6 2.5 copy-start.7
  351.2 1.6 copy-start.3
  352.8 1.3 copy-start.2
  400.1 14.6 %copy-start.4 = (f32[12,128,2,128]{3,1,2,0:T(8,128)S(1)}, f32[12,128,2,128]{3,1,2,0:T(8,128)}, u32[]{:S(2)}) copy-start(f32[12,128,2,128]{3,1,2,0:T(8,128)} %get-tuple-element.105) | copy-start | bytes 4718596
  407.7 14.5 %all-to-all-start.5 = ((bf16[1536,2,128]{2,1,0:T(2,128)(2,1)}), bf16[1536,2,128]{2,1,0:T(2,128)(2,1)}, u32[]{:S(2)}, u32[]{:S(2)}) async-start(bf16[1536,2,128]{2,1,0:T(2,128)(2,1)} %copy.222), calls=%async_computation.5 | async-start | bytes 1572864 | tf_op jit(solution)/shard_map/all_to_all | solution.py:146
  422.2 11.6 %all-to-all-start.6 = ((bf16[1536,2,128]{2,1,0:T(2,128)(2,1)}), bf16[1536,2,128]{2,1,0:T(2,128)(2,1)S(1)}, u32[]{:S(2)}, u32[]{:S(2)}) async-start(bf16[1536,2,128]{2,1,0:T(2,128)(2,1)} %copy.226), calls=%async_computation.6 | async-start | bytes 1572864 | tf_op jit(solution)/shard_map/all_to_all | solution.py:147
  433.8 10.9 %all-to-all-start.7 = ((bf16[1536,2,128]{2,1,0:T(2,128)(2,1)}), bf16[1536,2,128]{2,1,0:T(2,128)(2,1)S(1)}, u32[]{:S(2)}, u32[]{:S(2)}) async-start(bf16[1536,2,128]{2,1,0:T(2,128)(2,1)} %copy.230), calls=%async_computation.7 | async-start | bytes 1572864 | tf_op jit(solution)/shard_map/all_to_all | solution.py:148
  442.6 3.7 copy-start.9
  446.4 7.4 %copy-start.1 = (bf16[1,384,2048]{2,1,0:T(8,128)(2,1)S(1)}, bf16[1,384,2048]{2,1,0:T(8,128)(2,1)}, u32[]{:S(2)}) copy-start(bf16[1,384,2048]{2,1,0:T(8,128)(2,1)} %param.14) | copy-start | bytes 4718596
Sparse Core Ops, SparseCore 0:
  158.5 192.5 reduce-scatter.3
where the time goes:
time: 470 us; the launch traced here: 461 us
  local copies, waits for them, and re-layouts  242 us (51%)
  matrix products  65.9 us (14%)
  other arithmetic  52.2 us (11%)
  blocking collectives  36.3 us (8%)
  starting transfers between devices  30.6 us (7%)
  waiting for transfers between devices  19.2 us (4%)
  between operations  14.4 us (3%)
    gather x12, local copies, waits for them, and re-layouts, block_rows(): gathered = source_table[picked.reshape(-1)]  73.9 us
    scatter-add x3, other arithmetic, backward_step(): key_acc.at[flat_picks]  29.2 us
    all_to_all x1, blocking collectives, shards(): lax.all_to_all(attn_cot.reshape(tokens, HEADS, HEAD_SIZE), 'ctx', split_a...  23.1 us
    unnamed x24, local copies, waits for them, and re-layouts  20.8 us
    scatter-add x3, other arithmetic, backward_step(): value_acc.at[flat_picks]  19.5 us
    reshape x3, local copies, waits for them, and re-layouts, block_rows(): gathered.reshape((picked.shape[0], CHOSEN_BLOCKS * BLOCK_TOKENS) + source...  18.5 us
    transpose x3, local copies, waits for them, and re-layouts, backward_step(): jnp.einsum('ghqk,gqhd->gkhd', probs_narrow, cot_part, preferred_element_t...  16.1 us
    transpose x3, local copies, waits for them, and re-layouts, backward_step(): jnp.einsum('ghqk,gqhd->gkhd', score_cotangent, query_part, preferred_elem...  16 us
  transfers between devices with their start and end apart: 7, of which 4 were waited for; matrix products, arithmetic and copies ran while one was open for 56% of the time, Pallas kernels for 0%

commit v1 on v0

v1 whole, which is shorter than its diff:
```python
import functools
import math

import jax
import jax.numpy as jnp
from jax import lax
from jax.experimental import pallas as pl
from jax.experimental.pallas import tpu as pltpu
from jax.sharding import PartitionSpec as P

HEAD_SIZE = 128
BLOCK_TOKENS = 128
MESH = pl.DeviceIdType.MESH
BF16 = jnp.bfloat16
F32 = jnp.float32
VMEM_BYTES = 56 * 1024 * 1024


def mm(a, b, ca=1, cb=0):
    return lax.dot_general(a, b, (((ca,), (cb,)), ((), ())), preferred_element_type=F32)


def gather_kernel(
    n, q, k, v, w, oc, qo, ko, vo, co, oct_, wv, ocv, cotbuf, octv, send, recv, loc
):
    me = lax.axis_index("ctx")
    dp = lax.axis_index("dp")
    tokens = q.shape[0]
    hc = qo.shape[1]
    barrier = pltpu.get_barrier_semaphore()
    for d in range(1, n):
        pl.semaphore_signal(
            barrier, inc=1, device_id=(dp, lax.rem(me + d, n)), device_id_type=MESH
        )
    load_oc = pltpu.make_async_copy(oc, ocv, loc.at[0])
    load_oc.start()
    load_w = pltpu.make_async_copy(w, wv, loc.at[1])
    load_w.start()
    pl.semaphore_wait(barrier, n - 1)
    mine = pl.ds(pl.multiple_of(me * tokens, tokens), tokens)

    def cols(p):
        return pl.ds(pl.multiple_of(p * hc, hc), hc)

    remote, local = [], []
    for t, (src, dst) in enumerate(((q, qo), (k, ko), (v, vo))):
        for d in range(1, n):
            p = lax.rem(me + d, n)
            copy = pltpu.make_async_remote_copy(
                src.at[:, cols(p)], dst.at[mine, :], send.at[t, d], recv.at[t, d],
                device_id=(dp, p), device_id_type=MESH,
            )
            copy.start()
            remote.append(copy)
        copy = pltpu.make_async_copy(src.at[:, cols(me)], dst.at[mine, :], loc.at[2 + t])
        copy.start()
        local.append(copy)
    load_oc.wait()
    load_w.wait()
    for d in list(range(1, n)) + [0]:
        p = lax.rem(me + d, n)
        cotbuf[d] = mm(ocv[...], wv[:, cols(p)]).astype(BF16)
        if d:
            copy = pltpu.make_async_remote_copy(
                cotbuf.at[d], co.at[mine, :], send.at[3, d], recv.at[3, d],
                device_id=(dp, p), device_id_type=MESH,
            )
            remote.append(copy)
        else:
            copy = pltpu.make_async_copy(cotbuf.at[0], co.at[mine, :], loc.at[5])
            local.append(copy)
        copy.start()
    width = 256

    def flip(i, carry):
        at = pl.ds(pl.multiple_of(i * width, width), width)
        octv[at, :] = ocv[:, at].T
        return carry

    lax.fori_loop(0, oc.shape[1] // width, flip, 0)
    copy = pltpu.make_async_copy(octv, oct_, loc.at[6])
    copy.start()
    local.append(copy)
    for copy in local:
        copy.wait()
    for copy in remote:
        copy.wait()


def attention_kernel(heads, chosen, scale, picks, q, c, k, v, attn, dq, dk, dv, kt, vt, ka, va):
    step = pl.program_id(0)
    blocks = pl.num_programs(0)

    def rows(b):
        return pl.ds(pl.multiple_of(b * BLOCK_TOKENS, BLOCK_TOKENS), BLOCK_TOKENS)

    @pl.when(step == 0)
    def _():
        ka[...] = jnp.zeros_like(ka)
        va[...] = jnp.zeros_like(va)

        def turn(b, carry):
            for h in range(heads):
                hs = slice(h * HEAD_SIZE, (h + 1) * HEAD_SIZE)
                kt[h, b] = k[rows(b), hs].T
                vt[h, b] = v[rows(b), hs].T
            return carry

        lax.fori_loop(0, k.shape[0] // BLOCK_TOKENS, turn, 0)

    names = [picks[step, j] for j in range(chosen)]
    factor = scale * math.log2(math.e)
    for h in range(heads):
        hs = slice(h * HEAD_SIZE, (h + 1) * HEAD_SIZE)
        qh = q[:, hs]
        ch = c[:, hs]
        ks = jnp.concatenate([k[rows(b), hs] for b in names], axis=0)
        vs = jnp.concatenate([v[rows(b), hs] for b in names], axis=0)
        kts = jnp.concatenate([kt[h, b] for b in names], axis=1)
        vts = jnp.concatenate([vt[h, b] for b in names], axis=1)
        st = mm(ks, qh, 1, 1)
        top = jnp.max(st, axis=0, keepdims=True)
        e = jnp.exp2((st - top) * factor)
        inv = 1.0 / jnp.sum(e, axis=0, keepdims=True)
        pt = e * inv
        low = pt.astype(BF16)
        at = mm(vts, low).astype(BF16)
        a = at.T
        attn[:, hs] = a
        dot = jnp.sum(ch.astype(F32).T * at.astype(F32), axis=0, keepdims=True)
        dpt = mm(vs, ch, 1, 1)
        ds = (pt * (dpt - dot)).astype(BF16)
        dq[:, hs] = (mm(kts, ds) * scale).T.astype(BF16)
        dks = mm(ds, qh)
        dvs = mm(low, ch)
        for j, b in enumerate(names):
            part = slice(j * BLOCK_TOKENS, (j + 1) * BLOCK_TOKENS)
            ka[h, b] += dks[part]
            va[h, b] += dvs[part]

    @pl.when(step == blocks - 1)
    def _():
        def put(b, carry):
            for h in range(heads):
                hs = slice(h * HEAD_SIZE, (h + 1) * HEAD_SIZE)
                dk[rows(b), hs] = (ka[h, b] * scale).astype(BF16)
                dv[rows(b), hs] = va[h, b].astype(BF16)
            return carry

        lax.fori_loop(0, k.shape[0] // BLOCK_TOKENS, put, 0)


def scatter_kernel(
    n, nz, attn, dq, dk, dv, w, oct_, out, dqo, dko, dvo, wg,
    seq, wv, octv, acc, csend, crecv, zsend, rrecv, lrecv, xsend, xrecv,
    send, recv, loc, csem_s, csem_r, zsem_s, rsem_r, lsem_r, xsem_s, xsem_r,
):
    me = lax.axis_index("ctx")
    dp = lax.axis_index("dp")
    core = lax.rem(dp, 2)
    other = dp + 1 - 2 * core
    z = dp // 2
    tokens, total = seq.shape
    hc = attn.shape[1]
    sub = wg.shape[0]
    barrier = pltpu.get_barrier_semaphore()
    up = lax.rem(z + 1, nz) * 2 + core
    down = lax.rem(z + nz - 1, nz) * 2 + core
    for d in range(1, n):
        pl.semaphore_signal(
            barrier, inc=1, device_id=(dp, lax.rem(me + d, n)), device_id_type=MESH
        )
    for target in (other, up, down):
        pl.semaphore_signal(barrier, inc=1, device_id=(target, me), device_id_type=MESH)
    load_oct = pltpu.make_async_copy(oct_, octv, loc.at[0])
    load_oct.start()
    load_w = pltpu.make_async_copy(w, wv, loc.at[1])
    load_w.start()
    pl.semaphore_wait(barrier, n - 1 + 3)

    def rows(p):
        return pl.ds(pl.multiple_of(p * tokens, tokens), tokens)

    mycols = pl.ds(pl.multiple_of(me * hc, hc), hc)

    def spread(t, src, dst):
        remote = []
        for d in range(1, n):
            p = lax.rem(me + d, n)
            copy = pltpu.make_async_remote_copy(
                src.at[rows(p), :], dst.at[:, mycols], send.at[t, d], recv.at[t, d],
                device_id=(dp, p), device_id_type=MESH,
            )
            copy.start()
            remote.append(copy)
        own = pltpu.make_async_copy(src.at[rows(me), :], dst.at[:, mycols], loc.at[2 + t])
        own.start()
        return own, remote

    own, remote = spread(0, attn, seq)
    own.wait()
    for copy in remote:
        copy.wait_recv()
    grads = [spread(1 + t, s, o) for t, (s, o) in enumerate(((dq, dqo), (dk, dko), (dv, dvo)))]
    load_oct.wait()
    load_w.wait()

    def term(c, s, who):
        base = pl.multiple_of(((2 * c + who) * n + s) * sub, sub)
        return mm(octv[pl.ds(base, sub), :], seq[...])

    def core_copy(c):
        return pltpu.make_async_remote_copy(
            csend.at[c], crecv.at[c], csem_s.at[c], csem_r.at[c],
            device_id=(other, me), device_id_type=MESH,
        )

    def give(c, carry):
        for s in range(n):
            csend[c, s] = term(c, s, 1 - core).astype(BF16)
        core_copy(c).start()
        return carry

    lax.fori_loop(0, nz, give, 0)

    def keep(c, carry):
        for s in range(n):
            acc[c, s] = term(c, s, core)
        return carry

    lax.fori_loop(0, nz, keep, 0)

    def take(c, carry):
        core_copy(c).wait()
        for s in range(n):
            acc[c, s] += crecv[c, s].astype(F32)
        return carry

    lax.fori_loop(0, nz, take, 0)

    def right(c, s):
        return pltpu.make_async_remote_copy(
            zsend.at[c, s], rrecv.at[c, s], zsem_s.at[c, s], rsem_r.at[c, s],
            device_id=(up, me), device_id_type=MESH,
        )

    def left(c, s):
        return pltpu.make_async_remote_copy(
            zsend.at[c, s], lrecv.at[c, s], zsem_s.at[c, s], lsem_r.at[c, s],
            device_id=(down, me), device_id_type=MESH,
        )

    def line(u, carry):
        i = u - z

        @pl.when((i >= 0) & (i < (nz - 1 - z) * n))
        def _():
            c = nz - 1 - i // n
            s = lax.rem(i, n)

            @pl.when(z > 0)
            def _():
                right(c, s).wait_recv()
                acc[c, s] += rrecv[c, s].astype(F32)

            zsend[c, s] = acc[c, s].astype(BF16)
            right(c, s).start()

        j = u - (nz - 1 - z)

        @pl.when((j >= 0) & (j < z * n))
        def _():
            c = j // n
            s = lax.rem(j, n)

            @pl.when(z < nz - 1)
            def _():
                left(c, s).wait_recv()
                acc[c, s] += lrecv[c, s].astype(F32)

            zsend[c, s] = acc[c, s].astype(BF16)
            left(c, s).start()

        @pl.when(u < tiles)
        def _():
            at = pl.ds(pl.multiple_of(u * tile, tile), tile)
            out[:, at] = mm(seq[...], wv[at, :], 1, 1).astype(BF16)

        return carry

    tile = 256
    tiles = wv.shape[0] // tile
    lax.fori_loop(0, max((nz - 1) * n + nz, tiles), line, 0)

    def cross(s, slot):
        return pltpu.make_async_remote_copy(
            xsend.at[s], xrecv.at[slot], xsem_s.at[s], xsem_r.at[slot],
            device_id=(dp, s), device_id_type=MESH,
        )

    def finish(s, carry):
        @pl.when(z > 0)
        def _():
            right(z, s).wait_recv()
            acc[z, s] += rrecv[z, s].astype(F32)

        @pl.when(z < nz - 1)
        def _():
            left(z, s).wait_recv()
            acc[z, s] += lrecv[z, s].astype(F32)

        @pl.when(s != me)
        def _():
            xsend[s] = acc[z, s].astype(BF16)
            cross(s, me).start()

        return carry

    lax.fori_loop(0, n, finish, 0)
    wg[...] = acc[z, me]

    def gather(p, carry):
        @pl.when(p != me)
        def _():
            cross(p, p).wait_recv()
            wg[...] += xrecv[p].astype(F32)

        return carry

    lax.fori_loop(0, n, gather, 0)
    wg[...] = wg[...] * (1.0 / (2 * nz))

    def drain(s, carry):
        @pl.when(s != me)
        def _():
            cross(s, me).wait_send()

        for c in range(nz):
            @pl.when(z < c)
            def _():
                right(c, s).wait_send()

            @pl.when(z > c)
            def _():
                left(c, s).wait_send()

        return carry

    lax.fori_loop(0, n, drain, 0)
    for copy in remote:
        copy.wait_send()
    for own, copies in grads:
        own.wait()
        for copy in copies:
            copy.wait()


def shards(queries, keys, values, out_weight, out_cot, block_list):
    n = lax.axis_size("ctx")
    n_dp = lax.axis_size("dp")
    nz = n_dp // 2
    _, tokens, total = queries.shape
    model = out_weight.shape[0]
    hc = total // n
    heads = hc // HEAD_SIZE
    length = tokens * n
    blocks = length // BLOCK_TOKENS
    chosen = block_list.shape[1]
    sub = model // (n * n_dp)
    anyspec = pl.BlockSpec(memory_space=pl.ANY)
    vspec = pl.BlockSpec(memory_space=pltpu.VMEM)
    dma = pltpu.SemaphoreType.DMA

    byhead = jax.ShapeDtypeStruct((length, hc), BF16)
    bytoken = jax.ShapeDtypeStruct((tokens, total), BF16)
    qh, kh, vh, ch, oct_ = pl.pallas_call(
        functools.partial(gather_kernel, n),
        out_shape=(byhead, byhead, byhead, byhead, jax.ShapeDtypeStruct((model, tokens), BF16)),
        in_specs=[anyspec] * 5,
        out_specs=(anyspec,) * 5,
        scratch_shapes=[
            pltpu.VMEM((model, total), BF16),
            pltpu.VMEM((tokens, model), BF16),
            pltpu.VMEM((n, tokens, hc), BF16),
            pltpu.VMEM((model, tokens), BF16),
            dma((4, n)),
            dma((4, n)),
            dma((7,)),
        ],
        compiler_params=pltpu.CompilerParams(
            collective_id=0, has_side_effects=True, vmem_limit_bytes=VMEM_BYTES
        ),
    )(queries[0], keys[0], values[0], out_weight, out_cot[0])

    block = pl.BlockSpec((BLOCK_TOKENS, hc), lambda i, picks: (i, 0))
    whole = pl.BlockSpec((length, hc), lambda i, picks: (0, 0))
    attn, dqh, dkh, dvh = pl.pallas_call(
        functools.partial(attention_kernel, heads, chosen, 1.0 / math.sqrt(HEAD_SIZE)),
        out_shape=(byhead,) * 4,
        grid_spec=pltpu.PrefetchScalarGridSpec(
            num_scalar_prefetch=1,
            grid=(blocks,),
            in_specs=[block, block, whole, whole],
            out_specs=(block, block, whole, whole),
            scratch_shapes=[
                pltpu.VMEM((heads, blocks, HEAD_SIZE, BLOCK_TOKENS), BF16),
                pltpu.VMEM((heads, blocks, HEAD_SIZE, BLOCK_TOKENS), BF16),
                pltpu.VMEM((heads, blocks, BLOCK_TOKENS, HEAD_SIZE), F32),
                pltpu.VMEM((heads, blocks, BLOCK_TOKENS, HEAD_SIZE), F32),
            ],
        ),
        compiler_params=pltpu.CompilerParams(vmem_limit_bytes=VMEM_BYTES),
    )(block_list, qh, ch, kh, vh)

    lane = (nz, n, sub, total)
    out, dq, dk, dv, wg = pl.pallas_call(
        functools.partial(scatter_kernel, n, nz),
        out_shape=(
            jax.ShapeDtypeStruct((tokens, model), BF16),
            bytoken,
            bytoken,
            bytoken,
            jax.ShapeDtypeStruct((sub, total), F32),
        ),
        in_specs=[anyspec] * 6,
        out_specs=(vspec, anyspec, anyspec, anyspec, vspec),
        scratch_shapes=[
            pltpu.VMEM((tokens, total), BF16),
            pltpu.VMEM((model, total), BF16),
            pltpu.VMEM((model, tokens), BF16),
            pltpu.VMEM(lane, F32),
            pltpu.VMEM(lane, BF16),
            pltpu.VMEM(lane, BF16),
            pltpu.VMEM(lane, BF16),
            pltpu.VMEM(lane, BF16),
            pltpu.VMEM(lane, BF16),
            pltpu.VMEM(lane[1:], BF16),
            pltpu.VMEM(lane[1:], BF16),
            dma((4, n)),
            dma((4, n)),
            dma((6,)),
            dma((nz,)),
            dma((nz,)),
            dma((nz, n)),
            dma((nz, n)),
            dma((nz, n)),
            dma((n,)),
            dma((n,)),
        ],
        compiler_params=pltpu.CompilerParams(
            collective_id=1, has_side_effects=True, vmem_limit_bytes=VMEM_BYTES
        ),
    )(attn, dqh, dkh, dvh, out_weight, oct_)
    return out[None], dq[None], dk[None], dv[None], wg


def solution(mesh):
    part = P("dp", "ctx", None)
    return jax.shard_map(
        shards,
        mesh=mesh,
        in_specs=(part, part, part, P(), part, P()),
        out_specs=(part, part, part, part, P(("dp", "ctx"), None)),
        check_vma=False,
    )
```

time: 470 us -> 139 us (0.30); the launches traced: 461 us -> 138 us
  local copies, waits for them, and re-layouts: 242 us -> 7.56 us
  Pallas kernels: 0 us -> 130 us
  matrix products: 65.9 us -> 0 us
  other arithmetic: 52.2 us -> 0 us
  blocking collectives: 36.3 us -> 0 us
  starting transfers between devices: 30.6 us -> 0 us
  waiting for transfers between devices: 19.2 us -> 0 us
  between operations: 14.4 us -> 0.67 us
    pallas_call x0 -> x3, Pallas kernels: none -> 130 us  [the longest x1 62.7 us: shards(): pl.pallas_call(functools.partial(scatter_kernel, n, nz), out_shape=(jax.S...]
    reshape x22 -> x0, local copies, waits for them, and re-layouts: 75.8 us -> none  [the longest x3 18.5 us: block_rows(): gathered.reshape((picked.shape[0], CHOSEN_BLOCKS * BLOCK_TOKENS) + source...]
    gather x12 -> x0, local copies, waits for them, and re-layouts: 73.9 us -> none  [block_rows(): gathered = source_table[picked.reshape(-1)]]
    dot_general x24 -> x0, matrix products: 65.9 us -> none  [the longest x3 13.3 us: backward_step(): jnp.einsum('ghqk,gqhd->gkhd', score_cotangent, query_part, preferred_elem...]
    scatter-add x6 -> x0, other arithmetic: 48.7 us -> none  [the longest x3 29.2 us: backward_step(): key_acc.at[flat_picks]]
    all_to_all x2 -> x0, blocking collectives: 36.3 us -> none  [the longest x1 23.1 us: shards(): lax.all_to_all(attn_cot.reshape(tokens, HEADS, HEAD_SIZE), 'ctx', split_a...]
    transpose x6 -> x0, local copies, waits for them, and re-layouts: 32.1 us -> none  [the longest x3 16.1 us: backward_step(): jnp.einsum('ghqk,gqhd->gkhd', probs_narrow, cot_part, preferred_element_t...]
    all_to_all x6 -> x0, starting transfers between devices: 30.6 us -> none  [the longest x1 7.02 us: shards(): lax.all_to_all(query_grad_heads, 'ctx', split_axis=0, concat_axis=1, tile...]
  transfers between devices with their start and end apart: 7 -> 0, of which waited for: 4 -> 0; matrix products, arithmetic and copies ran while one was open for 56% -> 0% of each run, Pallas kernels for 0% -> 0%
where the time goes in v1:
time: 139 us; the launch traced here: 138 us
  Pallas kernels  130 us (94%)
  local copies, waits for them, and re-layouts  7.56 us (5%)
    pallas_call x1, Pallas kernels, shards(): pl.pallas_call(functools.partial(scatter_kernel, n, nz), out_shape=(jax.S...  62.7 us
    pallas_call x1, Pallas kernels, shards(): pl.pallas_call(functools.partial(gather_kernel, n), out_shape=(byhead, by...  37.8 us
    pallas_call x1, Pallas kernels, shards(): pl.pallas_call(functools.partial(attention_kernel, heads, chosen, 1.0 / m...  29.8 us
    unnamed x14, local copies, waits for them, and re-layouts  7.56 us

profile of v1, /device:TPU:14, one launch (start us, length us, event | category | flops | bytes accessed | tf_op | source)
XLA Modules:
  0.0 138.5 jit_solution(5294427371276912966)
XLA Ops:
  0.6 1.4 copy.11.picks
  2.0 37.8 %shard_map.101 = (bf16[1536,256]{1,0:T(8,128)(2,1)}, bf16[1536,256]{1,0:T(8,128)(2,1)}, bf16[1536,256]{1,0:T(8,128)(2,1)}, bf16[1536,256]{1,0:T(8,128)(2,1)}, bf16[2048,384]{1,0:T(8,128)(2,1)}) custom-call(bf16[384,1024]{1,0:T(8,128)(2,1)} %bitcast.13, bf16[384,1024]{1,0:T(8,128)(2,1)} %bitcast.14, bf16[384,1024]{1,0:T(8,128)(2,1)} %bitcast.15, ...), custom_call_target="tpu_custom_call" | custom-call | tf_op jit(solution)/shard_map/pallas_call | solution.py:376
  39.8 29.8 %shard_map.102 = (bf16[1536,256]{1,0:T(8,128)(2,1)}, bf16[1536,256]{1,0:T(8,128)(2,1)}, bf16[1536,256]{1,0:T(8,128)(2,1)}, bf16[1536,256]{1,0:T(8,128)(2,1)}) custom-call(s32[12,8]{1,0:T(8,128)} %copy.11.picks, bf16[1536,256]{1,0:T(8,128)(2,1)} %get-tuple-element.19.q, bf16[1536,256]{1,0:T(8,128)(2,1)} %get-tuple-element.20.c, ...), custom_call_target="tpu_custom_call" | custom-call | tf_op jit(solution)/shard_map/pallas_call | solution.py:397
  69.6 62.7 %shard_map.103 = (bf16[384,2048]{1,0:T(8,128)(2,1)}, bf16[384,1024]{1,0:T(8,128)(2,1)}, bf16[384,1024]{1,0:T(8,128)(2,1)}, bf16[384,1024]{1,0:T(8,128)(2,1)}, f32[64,1024]{1,0:T(8,128)}) custom-call(bf16[1536,256]{1,0:T(8,128)(2,1)} %get-tuple-element.23.attn, bf16[1536,256]{1,0:T(8,128)(2,1)} %get-tuple-element.24.dq, ...), custom_call_target="tpu_custom_call" | custom-call | tf_op jit(solution)/shard_map/pallas_call | solution.py:416
  132.3 0.0 copy-start.2
  132.3 0.0 copy-start.1
  132.3 2.8 %copy.17 = bf16[1,384,2048]{2,1,0:T(8,128)(2,1)} copy(bf16[1,384,2048]{2,1,0:T(8,128)(2,1)} %bitcast.8) | data formatting | bytes 3145728
  135.1 0.0 copy-done.2
  135.1 0.0 copy-start
  135.1 0.9 copy.18
  136.0 0.0 copy-done.1
  136.0 0.0 copy-start.3
  136.0 0.9 copy.19
  136.9 0.0 copy-done
  136.9 0.9 copy.20
  137.8 0.0 copy-done.3
  137.8 0.7 copy.21
Async XLA Ops:
  132.3 2.9 %copy-start.2 = (bf16[384,1024]{1,0:T(8,128)(2,1)S(1)}, bf16[384,1024]{1,0:T(8,128)(2,1)}, u32[]{:S(2)}) copy-start(bf16[384,1024]{1,0:T(8,128)(2,1)} %get-tuple-element.29) | copy-start | bytes 2359300
  132.3 3.7 %copy-start.1 = (bf16[384,1024]{1,0:T(8,128)(2,1)S(1)}, bf16[384,1024]{1,0:T(8,128)(2,1)}, u32[]{:S(2)}) copy-start(bf16[384,1024]{1,0:T(8,128)(2,1)} %get-tuple-element.30) | copy-start | bytes 2359300
  135.1 1.8 %copy-start = (bf16[384,1024]{1,0:T(8,128)(2,1)S(1)}, bf16[384,1024]{1,0:T(8,128)(2,1)}, u32[]{:S(2)}) copy-start(bf16[384,1024]{1,0:T(8,128)(2,1)} %get-tuple-element.31) | copy-start | bytes 2359300
  136.0 1.8 %copy-start.3 = (f32[64,1024]{1,0:T(8,128)S(1)}, f32[64,1024]{1,0:T(8,128)}, u32[]{:S(2)}) copy-start(f32[64,1024]{1,0:T(8,128)} %get-tuple-element.42) | copy-start | bytes 786436

commit v2 on v0

v2 whole, which is shorter than its diff:
```python
import functools
import math

import jax
import jax.numpy as jnp
from jax import lax
from jax.experimental import pallas as pl
from jax.experimental.pallas import tpu as pltpu
from jax.sharding import PartitionSpec as P

HEAD_SIZE = 128
BLOCK_TOKENS = 128
MESH = pl.DeviceIdType.MESH
BF16 = jnp.bfloat16
F32 = jnp.float32
VMEM_BYTES = 60 * 1024 * 1024


def mm(a, b, ca=1, cb=0):
    return lax.dot_general(a, b, (((ca,), (cb,)), ((), ())), preferred_element_type=F32)


def span(i, size):
    return pl.ds(pl.multiple_of(i * size, size), size)


def layer_kernel(n, nz, heads, names, picks, pos, q, k, v, w, oc, out, dqo, dko, dvo, wg, *scratch):
    r = dict(zip(names, scratch))
    me = lax.axis_index("ctx")
    dp = lax.axis_index("dp")
    core = lax.rem(dp, 2)
    other = dp + 1 - 2 * core
    z = dp // 2
    held = q.shape[0]
    tokens = held * BLOCK_TOKENS
    model = w.shape[0]
    blocks, chosen = picks.shape
    sub = wg.shape[0]
    scale = 1.0 / math.sqrt(HEAD_SIZE)
    factor = scale * math.log2(math.e)
    ocv, octv, wv, seq = r["ocv"], r["octv"], r["wv"], r["seq"]
    acc, ps, dss, kt, vt = r["acc"], r["ps"], r["dss"], r["kt"], r["vt"]
    loc = r["loc"]

    barrier = pltpu.get_barrier_semaphore()
    up = lax.rem(z + 1, nz) * 2 + core
    down = lax.rem(z + nz - 1, nz) * 2 + core
    for d in range(1, n):
        pl.semaphore_signal(
            barrier, inc=1, device_id=(dp, lax.rem(me + d, n)), device_id_type=MESH
        )
    for target in (other, up, down):
        pl.semaphore_signal(barrier, inc=1, device_id=(target, me), device_id_type=MESH)
    load_oc = pltpu.make_async_copy(oc, ocv, loc.at[0])
    load_oc.start()
    load_w = []
    for h in range(heads):
        for p in range(n):
            copy = pltpu.make_async_copy(
                w.at[:, pl.ds((p * heads + h) * HEAD_SIZE, HEAD_SIZE)],
                wv.at[h, :, pl.ds(p * HEAD_SIZE, HEAD_SIZE)],
                r["wsem"].at[h, p],
            )
            copy.start()
            load_w.append(copy)
    pl.semaphore_wait(barrier, n - 1 + 3)

    def trade(src_of, dst, send, recv, own_sem):
        remote = []
        for d in range(1, n):
            p = lax.rem(me + d, n)
            copy = pltpu.make_async_remote_copy(
                src_of(p, d), dst, send.at[d], recv.at[d],
                device_id=(dp, p), device_id_type=MESH,
            )
            copy.start()
            remote.append(copy)
        own = pltpu.make_async_copy(src_of(me, 0), dst, own_sem)
        own.start()
        return own, remote

    def column(p, h):
        return span(p * heads + h, HEAD_SIZE)

    mine = pl.ds(me * held, held)

    def send_rows(h):
        return [
            trade(
                lambda p, d, x=x: x.at[:, :, column(p, h)], r[f"{t}{h}"].at[mine],
                r["in_s"].at[h, i], r["in_r"].at[h, i], r["in_l"].at[h, i],
            )
            for i, (t, x) in enumerate((("q", q), ("k", k), ("v", v)))
        ]

    def send_cot(h):
        return [
            trade(
                lambda p, d: r["cotbuf"].at[h, d], r[f"c{h}"].at[mine],
                r["in_s"].at[h, 3], r["in_r"].at[h, 3], r["in_l"].at[h, 3],
            )
        ]

    def work_cot(h):
        for d in range(n):
            p = lax.rem(me + d, n)
            r["cotbuf"][h, d] = (
                mm(ocv[...], wv[h, :, span(p, HEAD_SIZE)])
                .astype(BF16)
                .reshape(held, BLOCK_TOKENS, HEAD_SIZE)
            )

    sent = []

    def arrive(trades):
        for own, remote in trades:
            own.wait()
            for copy in remote:
                copy.wait_recv()
            sent.extend(remote)

    coming = send_rows(0)
    load_oc.wait()
    for copy in load_w:
        copy.wait()
    work_cot(0)
    coming += send_cot(0)
    for h in range(1, heads):
        work_cot(h)

    def flip(i, carry):
        octv[span(i, 256), :] = ocv[:, span(i, 256)].T
        return carry

    lax.fori_loop(0, model // 256, flip, 0)

    def clear(i, carry):
        ps[i, chosen] = jnp.zeros((BLOCK_TOKENS, BLOCK_TOKENS), BF16)
        dss[i, chosen] = jnp.zeros((BLOCK_TOKENS, BLOCK_TOKENS), BF16)
        return carry

    lax.fori_loop(0, blocks, clear, 0)

    def attend(h, i):
        at = span(i, BLOCK_TOKENS)
        kh, vh = r[f"k{h}"], r[f"v{h}"]
        qi = r[f"q{h}"][i]
        ci = r[f"c{h}"][i]
        ids = [picks[i, j] for j in range(chosen)]
        ks = jnp.concatenate([kh[b] for b in ids], axis=0)
        vs = jnp.concatenate([vh[b] for b in ids], axis=0)
        kts = jnp.concatenate([kt[b] for b in ids], axis=1)
        vts = jnp.concatenate([vt[b] for b in ids], axis=1)
        st = mm(ks, qi, 1, 1)
        dpt = mm(vs, ci, 1, 1)
        top = jnp.max(st, axis=0, keepdims=True)
        e = jnp.exp2((st - top) * factor)
        inv = 1.0 / jnp.sum(e, axis=0, keepdims=True)
        pt = e * inv
        low = pt.astype(BF16)
        a = mm(vts, low).astype(BF16)
        r["attn"][h, at, :] = a.T
        dot = jnp.sum(ci.astype(F32).T * a.astype(F32), axis=0, keepdims=True)
        ds = (pt * (dpt - dot)).astype(BF16)
        r["dq"][h, at, :] = (mm(kts, ds) * scale).T.astype(BF16)
        for j in range(chosen):
            part = slice(j * BLOCK_TOKENS, (j + 1) * BLOCK_TOKENS)
            ps[i, j] = low[part]
            dss[i, j] = ds[part]

    def collect(h):
        def body(j, carry):
            at = span(j, BLOCK_TOKENS)
            slots = [pos[i, j] for i in range(blocks)]
            dst = jnp.concatenate([dss[i, s] for i, s in enumerate(slots)], axis=1)
            r["dk"][h, at, :] = (mm(dst, r[f"q{h}"][...].reshape(-1, HEAD_SIZE)) * scale).astype(BF16)
            pst = jnp.concatenate([ps[i, s] for i, s in enumerate(slots)], axis=1)
            r["dv"][h, at, :] = mm(pst, r[f"c{h}"][...].reshape(-1, HEAD_SIZE)).astype(BF16)
            return carry

        lax.fori_loop(0, blocks, body, 0)

    def turn(h):
        def body(b, carry):
            kt[b] = r[f"k{h}"][b].T
            vt[b] = r[f"v{h}"][b].T
            return carry

        lax.fori_loop(0, blocks, body, 0)

    def send_attn(h):
        return [
            trade(
                lambda p, d: r["attn"].at[h, span(p, tokens), :],
                seq.at[h, :, span(me, HEAD_SIZE)],
                r["out_s"].at[h, 0], r["out_r"].at[h, 0], r["out_l"].at[h, 0],
            )
        ]

    def send_grads(h):
        return [
            trade(
                lambda p, d, t=t: r[t].at[h, span(p, tokens), :], o.at[:, column(me, h)],
                r["out_s"].at[h, i], r["out_r"].at[h, i], r["out_l"].at[h, i],
            )
            for i, t, o in ((1, "dq", dqo), (2, "dk", dko), (3, "dv", dvo))
        ]

    def term(h, c, s, who):
        return mm(octv[span((2 * c + who) * n + s, sub), :], seq[h])

    def core_copy(h, c):
        return pltpu.make_async_remote_copy(
            r["csend"].at[h, c], r["crecv"].at[h, c], r["csem_s"].at[h, c], r["csem_r"].at[h, c],
            device_id=(other, me), device_id_type=MESH,
        )

    def give(h):
        def body(c, carry):
            for s in range(n):
                r["csend"][h, c, s] = term(h, c, s, 1 - core).astype(BF16)
            core_copy(h, c).start()
            return carry

        lax.fori_loop(0, nz, body, 0)

        def keep(c, carry):
            for s in range(n):
                acc[h, c, s] = term(h, c, s, core)
            return carry

        lax.fori_loop(0, nz, keep, 0)

    def take(h):
        def body(c, carry):
            core_copy(h, c).wait()
            for s in range(n):
                acc[h, c, s] += r["crecv"][h, c, s].astype(F32)
            return carry

        lax.fori_loop(0, nz, body, 0)

    def hop(h, c, s, buf, sem, target):
        return pltpu.make_async_remote_copy(
            r["zsend"].at[h, c, s], r[buf].at[h, c, s], r["zsem"].at[h, c, s],
            r[sem].at[h, c, s], device_id=(target, me), device_id_type=MESH,
        )

    def right(h, c, s):
        return hop(h, c, s, "rrecv", "rsem", up)

    def left(h, c, s):
        return hop(h, c, s, "lrecv", "lsem", down)

    def line(h, u):
        i = u - z

        @pl.when((i >= 0) & (i < (nz - 1 - z) * n))
        def _():
            c = nz - 1 - i // n
            s = lax.rem(i, n)

            @pl.when(z > 0)
            def _():
                right(h, c, s).wait_recv()
                acc[h, c, s] += r["rrecv"][h, c, s].astype(F32)

            r["zsend"][h, c, s] = acc[h, c, s].astype(BF16)
            right(h, c, s).start()

        j = u - (nz - 1 - z)

        @pl.when((j >= 0) & (j < z * n))
        def _():
            c = j // n
            s = lax.rem(j, n)

            @pl.when(z < nz - 1)
            def _():
                left(h, c, s).wait_recv()
                acc[h, c, s] += r["lrecv"][h, c, s].astype(F32)

            r["zsend"][h, c, s] = acc[h, c, s].astype(BF16)
            left(h, c, s).start()

    hops = (nz - 1) * n + nz

    def lines(h, first):
        def body(u, carry):
            line(h, u)
            return carry

        lax.fori_loop(first, hops, body, 0)

    def cross(h, s, slot):
        return pltpu.make_async_remote_copy(
            r["xsend"].at[h, s], r["xrecv"].at[h, slot], r["xsem_s"].at[h, s],
            r["xsem_r"].at[h, slot], device_id=(dp, s), device_id_type=MESH,
        )

    def finish(h):
        def body(s, carry):
            @pl.when(z > 0)
            def _():
                right(h, z, s).wait_recv()
                acc[h, z, s] += r["rrecv"][h, z, s].astype(F32)

            @pl.when(z < nz - 1)
            def _():
                left(h, z, s).wait_recv()
                acc[h, z, s] += r["lrecv"][h, z, s].astype(F32)

            @pl.when(s != me)
            def _():
                r["xsend"][h, s] = acc[h, z, s].astype(BF16)
                cross(h, s, me).start()

            return carry

        lax.fori_loop(0, n, body, 0)

    def total(h):
        r["sum"][...] = acc[h, z, me]

        def body(p, carry):
            @pl.when(p != me)
            def _():
                cross(h, p, p).wait_recv()
                r["sum"][...] += r["xrecv"][h, p].astype(F32)

            return carry

        lax.fori_loop(0, n, body, 0)
        for p in range(n):
            wg[:, pl.ds((p * heads + h) * HEAD_SIZE, HEAD_SIZE)] = r["sum"][
                :, p * HEAD_SIZE : (p + 1) * HEAD_SIZE
            ] * (1.0 / (2 * nz))

    def drain(h):
        def body(s, carry):
            @pl.when(s != me)
            def _():
                cross(h, s, me).wait_send()

            for c in range(nz):
                @pl.when(z < c)
                def _():
                    right(h, c, s).wait_send()

                @pl.when(z > c)
                def _():
                    left(h, c, s).wait_send()

            return carry

        lax.fori_loop(0, n, body, 0)

    pair = math.gcd(blocks, 2)
    turns = blocks // pair
    begin = turns // 2
    per = 3
    done = min(hops, (turns - begin) * per)
    going, attn_going = [], []
    for h in range(heads):
        arrive(coming)
        if h + 1 < heads:
            coming = send_rows(h + 1) + send_cot(h + 1)
        turn(h)

        def body(t, carry, h=h):
            for b in range(pair):
                attend(h, t * pair + b)
            if h > 0:
                @pl.when(t == begin - 1)
                def _():
                    give(h - 1)

                @pl.when(t == begin)
                def _():
                    take(h - 1)

                @pl.when(t >= begin)
                def _():
                    for x in range(per):
                        line(h - 1, (t - begin) * per + x)

            return carry

        if h > 0:
            split = min(begin - 1, 2)
            lax.fori_loop(0, split, body, 0)
            arrive(attn_going)
            lax.fori_loop(split, turns, body, 0)
        else:
            lax.fori_loop(0, turns, body, 0)
        attn_going = send_attn(h)
        collect(h)
        if h > 0:
            lines(h - 1, done)
            finish(h - 1)
        if h + 1 < heads:
            going += send_grads(h)
    arrive(attn_going)
    going += send_grads(heads - 1)
    give(heads - 1)
    tile = 256

    def project(i, carry):
        at = span(i, tile)
        part = mm(seq[0], wv[0, at, :], 1, 1)
        for h in range(1, heads):
            part += mm(seq[h], wv[h, at, :], 1, 1)
        out[:, at] = part.astype(BF16)
        return carry

    take(heads - 1)

    def both(u, carry):
        line(heads - 1, u)

        @pl.when(u < model // tile)
        def _():
            project(u, 0)

        return carry

    lax.fori_loop(0, max(hops, model // tile), both, 0)
    finish(heads - 1)
    for h in range(heads):
        total(h)
    for h in range(heads):
        drain(h)
    arrive(going)
    for copy in sent:
        copy.wait_send()


def shards(queries, keys, values, out_weight, out_cot, block_list):
    n = lax.axis_size("ctx")
    n_dp = lax.axis_size("dp")
    nz = n_dp // 2
    _, tokens, total = queries.shape
    model = out_weight.shape[0]
    heads = total // n // HEAD_SIZE
    length = tokens * n
    held = tokens // BLOCK_TOKENS
    blocks, chosen = block_list.shape
    sub = model // (n * n_dp)
    anyspec = pl.BlockSpec(memory_space=pl.ANY)
    vspec = pl.BlockSpec(memory_space=pltpu.VMEM)
    sspec = pl.BlockSpec(memory_space=pltpu.SMEM)
    dma = pltpu.SemaphoreType.DMA

    listed = block_list[:, :, None] == jnp.arange(blocks, dtype=jnp.int32)
    slot = jnp.arange(chosen, dtype=jnp.int32)[None, :, None] - chosen
    pos = chosen + jnp.sum(jnp.where(listed, slot, 0), axis=1)

    width = n * HEAD_SIZE
    lane = (heads, nz, n, sub, width)
    cross = (heads, n, sub, width)
    byhead = (heads, length, HEAD_SIZE)
    scratch = {
        "ocv": pltpu.VMEM((tokens, model), BF16),
        "octv": pltpu.VMEM((model, tokens), BF16),
        "wv": pltpu.VMEM((heads, model, width), BF16),
        "seq": pltpu.VMEM((heads, tokens, width), BF16),
        "cotbuf": pltpu.VMEM((heads, n, held, BLOCK_TOKENS, HEAD_SIZE), BF16),
        "attn": pltpu.VMEM(byhead, BF16),
        "dq": pltpu.VMEM(byhead, BF16),
        "dk": pltpu.VMEM(byhead, BF16),
        "dv": pltpu.VMEM(byhead, BF16),
        "ps": pltpu.VMEM((blocks, chosen + 1, BLOCK_TOKENS, BLOCK_TOKENS), BF16),
        "dss": pltpu.VMEM((blocks, chosen + 1, BLOCK_TOKENS, BLOCK_TOKENS), BF16),
        "kt": pltpu.VMEM((blocks, HEAD_SIZE, BLOCK_TOKENS), BF16),
        "vt": pltpu.VMEM((blocks, HEAD_SIZE, BLOCK_TOKENS), BF16),
        "acc": pltpu.VMEM(lane, F32),
        "sum": pltpu.VMEM((sub, width), F32),
        "csend": pltpu.VMEM(lane, BF16),
        "crecv": pltpu.VMEM(lane, BF16),
        "zsend": pltpu.VMEM(lane, BF16),
        "rrecv": pltpu.VMEM(lane, BF16),
        "lrecv": pltpu.VMEM(lane, BF16),
        "xsend": pltpu.VMEM(cross, BF16),
        "xrecv": pltpu.VMEM(cross, BF16),
        "loc": dma((1,)),
        "wsem": dma((heads, n)),
        "in_s": dma((heads, 4, n)),
        "in_r": dma((heads, 4, n)),
        "in_l": dma((heads, 4)),
        "out_s": dma((heads, 4, n)),
        "out_r": dma((heads, 4, n)),
        "out_l": dma((heads, 4)),
        "csem_s": dma((heads, nz)),
        "csem_r": dma((heads, nz)),
        "zsem": dma((heads, nz, n)),
        "rsem": dma((heads, nz, n)),
        "lsem": dma((heads, nz, n)),
        "xsem_s": dma((heads, n)),
        "xsem_r": dma((heads, n)),
    }
    for h in range(heads):
        for t in "qkvc":
            scratch[f"{t}{h}"] = pltpu.VMEM((blocks, BLOCK_TOKENS, HEAD_SIZE), BF16)
    rows = [x.reshape(held, BLOCK_TOKENS, total) for x in (queries, keys, values)]
    bytoken = jax.ShapeDtypeStruct((tokens, total), BF16)
    out, dq, dk, dv, wg = pl.pallas_call(
        functools.partial(layer_kernel, n, nz, heads, tuple(scratch)),
        out_shape=(
            jax.ShapeDtypeStruct((tokens, model), BF16),
            bytoken,
            bytoken,
            bytoken,
            jax.ShapeDtypeStruct((sub, total), F32),
        ),
        in_specs=[sspec] * 2 + [anyspec] * 5,
        out_specs=(vspec, anyspec, anyspec, anyspec, vspec),
        scratch_shapes=list(scratch.values()),
        compiler_params=pltpu.CompilerParams(
            collective_id=0, has_side_effects=True, vmem_limit_bytes=VMEM_BYTES
        ),
    )(block_list, pos, *rows, out_weight, out_cot[0])
    return out[None], dq[None], dk[None], dv[None], wg


def solution(mesh):
    part = P("dp", "ctx", None)
    return jax.shard_map(
        shards,
        mesh=mesh,
        in_specs=(part, part, part, P(), part, P()),
        out_specs=(part, part, part, part, P(("dp", "ctx"), None)),
        check_vma=False,
    )
```

time: 470 us -> 117 us (0.25); the launches traced: 461 us -> 117 us
  local copies, waits for them, and re-layouts: 242 us -> 7.46 us
  Pallas kernels: 0 us -> 108 us
  matrix products: 65.9 us -> 0 us
  other arithmetic: 52.2 us -> 0.7 us
  blocking collectives: 36.3 us -> 0 us
  starting transfers between devices: 30.6 us -> 0 us
  waiting for transfers between devices: 19.2 us -> 0 us
  between operations: 14.4 us -> 0.67 us
    pallas_call x0 -> x1, Pallas kernels: none -> 108 us  [shards(): pl.pallas_call(functools.partial(layer_kernel, n, nz, heads, tuple(scratc...]
    reshape x22 -> x0, local copies, waits for them, and re-layouts: 75.8 us -> none  [the longest x3 18.5 us: block_rows(): gathered.reshape((picked.shape[0], CHOSEN_BLOCKS * BLOCK_TOKENS) + source...]
    gather x12 -> x0, local copies, waits for them, and re-layouts: 73.9 us -> none  [block_rows(): gathered = source_table[picked.reshape(-1)]]
    dot_general x24 -> x0, matrix products: 65.9 us -> none  [the longest x3 13.3 us: backward_step(): jnp.einsum('ghqk,gqhd->gkhd', score_cotangent, query_part, preferred_elem...]
    scatter-add x6 -> x0, other arithmetic: 48.7 us -> none  [the longest x3 29.2 us: backward_step(): key_acc.at[flat_picks]]
    all_to_all x2 -> x0, blocking collectives: 36.3 us -> none  [the longest x1 23.1 us: shards(): lax.all_to_all(attn_cot.reshape(tokens, HEADS, HEAD_SIZE), 'ctx', split_a...]
    transpose x6 -> x0, local copies, waits for them, and re-layouts: 32.1 us -> none  [the longest x3 16.1 us: backward_step(): jnp.einsum('ghqk,gqhd->gkhd', probs_narrow, cot_part, preferred_element_t...]
    all_to_all x6 -> x0, starting transfers between devices: 30.6 us -> none  [the longest x1 7.02 us: shards(): lax.all_to_all(query_grad_heads, 'ctx', split_axis=0, concat_axis=1, tile...]
  transfers between devices with their start and end apart: 7 -> 0, of which waited for: 4 -> 0; matrix products, arithmetic and copies ran while one was open for 56% -> 0% of each run, Pallas kernels for 0% -> 0%
where the time goes in v2:
time: 117 us
  Pallas kernels  108 us (92%)
  local copies, waits for them, and re-layouts  7.46 us (6%)
    pallas_call x1, Pallas kernels, shards(): pl.pallas_call(functools.partial(layer_kernel, n, nz, heads, tuple(scratc...  108 us
    unnamed x16, local copies, waits for them, and re-layouts  7.46 us

profile of v2, /device:TPU:14, one launch (start us, length us, event | category | flops | bytes accessed | tf_op | source)
XLA Modules:
  0.0 116.6 jit_solution(5810590823434306677)
XLA Ops:
  0.6 0.8 copy.14.picks
  1.4 0.0 copy-start.4
  1.4 0.1 select_reduce_fusion
  1.5 0.6 broadcast_add_fusion.pos
  2.1 0.0 copy-done.4
  2.1 107.7 %shard_map.101 = (bf16[384,2048]{1,0:T(8,128)(2,1)}, bf16[384,1024]{1,0:T(8,128)(2,1)}, bf16[384,1024]{1,0:T(8,128)(2,1)}, bf16[384,1024]{1,0:T(8,128)(2,1)}, f32[64,1024]{1,0:T(8,128)}) custom-call(s32[12,8]{1,0:T(8,128)} %copy-done.4, s32[12,12]{1,0:T(8,128)} %broadcast_add_fusion.pos, bf16[3,128,1024]{2,1,0:T(8,128)(2,1)} %bitcast.13, ...), custom_call_target="tpu_custom_call" | custom-call | tf_op jit(solution)/shard_map/pallas_call | solution.py:506
  109.9 0.0 copy-start.2
  109.9 2.8 %copy.20 = bf16[1,384,2048]{2,1,0:T(8,128)(2,1)} copy(bf16[1,384,2048]{2,1,0:T(8,128)(2,1)} %bitcast.8) | data formatting | bytes 3145728
  112.7 0.0 copy-done.2
  112.7 0.0 copy-start.1
  112.7 0.0 copy-start
  112.7 0.9 copy.21
  113.6 0.5 copy-done.1
  114.1 0.0 copy-start.3
  114.1 0.9 copy.22
  115.0 0.0 copy-done
  115.0 0.9 copy.23
  115.9 0.0 copy-done.3
  115.9 0.7 copy.24
  (1 shorter events, 0.0 us)
Async XLA Ops:
  1.4 0.7 copy-start.4
  109.9 2.8 %copy-start.2 = (bf16[384,1024]{1,0:T(8,128)(2,1)S(1)}, bf16[384,1024]{1,0:T(8,128)(2,1)}, u32[]{:S(2)}) copy-start(bf16[384,1024]{1,0:T(8,128)(2,1)} %get-tuple-element.11) | copy-start | bytes 2359300
  112.7 1.4 %copy-start.1 = (bf16[384,1024]{1,0:T(8,128)(2,1)S(1)}, bf16[384,1024]{1,0:T(8,128)(2,1)}, u32[]{:S(2)}) copy-start(bf16[384,1024]{1,0:T(8,128)(2,1)} %get-tuple-element.12) | copy-start | bytes 2359300
  112.7 2.3 %copy-start = (bf16[384,1024]{1,0:T(8,128)(2,1)S(1)}, bf16[384,1024]{1,0:T(8,128)(2,1)}, u32[]{:S(2)}) copy-start(bf16[384,1024]{1,0:T(8,128)(2,1)} %get-tuple-element.13) | copy-start | bytes 2359300
  114.1 1.8 %copy-start.3 = (f32[64,1024]{1,0:T(8,128)S(1)}, f32[64,1024]{1,0:T(8,128)}, u32[]{:S(2)}) copy-start(f32[64,1024]{1,0:T(8,128)} %get-tuple-element.24) | copy-start | bytes 786436

commit v3 on v2

--- a/solution.py
+++ b/solution.py
@@ -168,17 +168,27 @@
             ps[i, j] = low[part]
             dss[i, j] = ds[part]
 
+    group = math.gcd(blocks, 4)
+
     def collect(h):
-        def body(j, carry):
-            at = span(j, BLOCK_TOKENS)
-            slots = [pos[i, j] for i in range(blocks)]
-            dst = jnp.concatenate([dss[i, s] for i, s in enumerate(slots)], axis=1)
+        def wide(kept, g):
+            return jnp.concatenate(
+                [
+                    jnp.concatenate([kept[i, pos[i, g * group + x]] for i in range(blocks)], axis=1)
+                    for x in range(group)
+                ],
+                axis=0,
+            )
+
+        def body(g, carry):
+            at = span(g, group * BLOCK_TOKENS)
+            dst = wide(dss, g)
             r["dk"][h, at, :] = (mm(dst, r[f"q{h}"][...].reshape(-1, HEAD_SIZE)) * scale).astype(BF16)
-            pst = jnp.concatenate([ps[i, s] for i, s in enumerate(slots)], axis=1)
+            pst = wide(ps, g)
             r["dv"][h, at, :] = mm(pst, r[f"c{h}"][...].reshape(-1, HEAD_SIZE)).astype(BF16)
             return carry
 
-        lax.fori_loop(0, blocks, body, 0)
+        lax.fori_loop(0, blocks // group, body, 0)
 
     def turn(h):
         def body(b, carry):
@@ -206,8 +216,8 @@
             for i, t, o in ((1, "dq", dqo), (2, "dk", dko), (3, "dv", dvo))
         ]
 
-    def term(h, c, s, who):
-        return mm(octv[span((2 * c + who) * n + s, sub), :], seq[h])
+    def term(h, c, who):
+        return mm(octv[span(2 * c + who, n * sub), :], seq[h]).reshape(n, sub, -1)
 
     def core_copy(h, c):
         return pltpu.make_async_remote_copy(
@@ -217,16 +227,14 @@
 
     def give(h):
         def body(c, carry):
-            for s in range(n):
-                r["csend"][h, c, s] = term(h, c, s, 1 - core).astype(BF16)
+            r["csend"][h, c] = term(h, c, 1 - core).astype(BF16)
             core_copy(h, c).start()
             return carry
 
         lax.fori_loop(0, nz, body, 0)
 
         def keep(c, carry):
-            for s in range(n):
-                acc[h, c, s] = term(h, c, s, core)
+            acc[h, c] = term(h, c, core)
             return carry
 
         lax.fori_loop(0, nz, keep, 0)

time: 117 us -> 116 us (level)
  no operation moved by 1% of the time
where the time goes in v3:
time: 116 us
  Pallas kernels  107 us (92%)
  local copies, waits for them, and re-layouts  7.46 us (6%)
    pallas_call x1, Pallas kernels, shards(): pl.pallas_call(functools.partial(layer_kernel, n, nz, heads, tuple(scratc...  107 us
    unnamed x16, local copies, waits for them, and re-layouts  7.46 us

profile of v3, /device:TPU:14, one launch (start us, length us, event | category | flops | bytes accessed | tf_op | source)
XLA Modules:
  0.0 116.1 jit_solution(2014867263521158485)
XLA Ops:
  0.6 0.8 copy.14.picks
  1.4 0.0 copy-start.4
  1.4 0.1 select_reduce_fusion
  1.5 0.6 broadcast_add_fusion.pos
  2.1 0.0 copy-done.4
  2.1 107.3 %shard_map.101 = (bf16[384,2048]{1,0:T(8,128)(2,1)}, bf16[384,1024]{1,0:T(8,128)(2,1)}, bf16[384,1024]{1,0:T(8,128)(2,1)}, bf16[384,1024]{1,0:T(8,128)(2,1)}, f32[64,1024]{1,0:T(8,128)}) custom-call(s32[12,8]{1,0:T(8,128)} %copy-done.4, s32[12,12]{1,0:T(8,128)} %broadcast_add_fusion.pos, bf16[3,128,1024]{2,1,0:T(8,128)(2,1)} %bitcast.13, ...), custom_call_target="tpu_custom_call" | custom-call | tf_op jit(solution)/shard_map/pallas_call | solution.py:514
  109.4 0.0 copy-start.2
  109.4 2.8 %copy.20 = bf16[1,384,2048]{2,1,0:T(8,128)(2,1)} copy(bf16[1,384,2048]{2,1,0:T(8,128)(2,1)} %bitcast.8) | data formatting | bytes 3145728
  112.2 0.0 copy-done.2
  112.2 0.0 copy-start.1
  112.2 0.0 copy-start
  112.2 0.9 copy.21
  113.1 0.5 copy-done.1
  113.6 0.0 copy-start.3
  113.6 0.9 copy.22
  114.5 0.0 copy-done
  114.5 0.9 copy.23
  115.4 0.0 copy-done.3
  115.4 0.7 copy.24
  (1 shorter events, 0.0 us)
Async XLA Ops:
  1.4 0.7 copy-start.4
  109.4 2.8 %copy-start.2 = (bf16[384,1024]{1,0:T(8,128)(2,1)S(1)}, bf16[384,1024]{1,0:T(8,128)(2,1)}, u32[]{:S(2)}) copy-start(bf16[384,1024]{1,0:T(8,128)(2,1)} %get-tuple-element.11) | copy-start | bytes 2359300
  112.2 1.4 %copy-start.1 = (bf16[384,1024]{1,0:T(8,128)(2,1)S(1)}, bf16[384,1024]{1,0:T(8,128)(2,1)}, u32[]{:S(2)}) copy-start(bf16[384,1024]{1,0:T(8,128)(2,1)} %get-tuple-element.12) | copy-start | bytes 2359300
  112.2 2.3 %copy-start = (bf16[384,1024]{1,0:T(8,128)(2,1)S(1)}, bf16[384,1024]{1,0:T(8,128)(2,1)}, u32[]{:S(2)}) copy-start(bf16[384,1024]{1,0:T(8,128)(2,1)} %get-tuple-element.13) | copy-start | bytes 2359300
  113.6 1.8 %copy-start.3 = (f32[64,1024]{1,0:T(8,128)S(1)}, f32[64,1024]{1,0:T(8,128)}, u32[]{:S(2)}) copy-start(f32[64,1024]{1,0:T(8,128)} %get-tuple-element.24) | copy-start | bytes 786436
